TPU v7x, 32 devices: a whole 2x2x4 slice. The times are simulated.
32 devices in a mesh: groups: 2 (over y), col: 8 (over z, x), row: 2 (over core).
Axes of the slice: x: 2, y: 2, z: 4, core: 2. Of those that a mesh axis runs over, the one named last changes fastest.
Arguments:
- tokens: bfloat16 [640, 8192], P(('groups', 'row'), 'col'), parts along dimension 0, may hold values from -6 to 6
- gate_weight: bfloat16 [8192, 2, 13312], P('row', None, 'col'), may hold values from -0.0625 to 0.0625
- up_weight: bfloat16 [8192, 2, 13312], P('row', None, 'col'), may hold values from -0.0625 to 0.0625
- down_weight: bfloat16 [2, 13312, 8192], P('row', None, 'col'), may hold values from -0.0390625 to 0.0390625
Outputs:
- output_rows: bfloat16 [640, 8192], P(('groups', 'row'), 'col'), parts along dimension 0
There are 2 independent parts, one for each index of `groups`. A program takes and returns all parts, laid end to end along the dimension named above; an argument that names none is the same for every part. Nothing has to cross between parts.
All inputs are finite; a program needn't handle non-finite values.
Results may differ from a plain program's by a relative error of at most 0.006.
Values may be sent and summed in bfloat16 or wider, within the bound.
A program may use at most 576 MiB of HBM per device.

v0:
```python
import jax
import jax.numpy as jnp
from jax import lax
from jax.sharding import PartitionSpec as P


def local(tokens, gate_weight, up_weight, down_weight):
    features = lax.all_gather(tokens, "col", axis=1, tiled=True)
    local_rows = features.shape[0]
    gate_local = gate_weight.reshape(gate_weight.shape[0], -1)
    up_local = up_weight.reshape(up_weight.shape[0], -1)
    gate_proj = jnp.dot(
        features,
        lax.all_gather(gate_local, "row", axis=0, tiled=True),
        preferred_element_type=jnp.float32,
    )
    up_proj = jnp.dot(
        features,
        lax.all_gather(up_local, "row", axis=0, tiled=True),
        preferred_element_type=jnp.float32,
    )
    hidden = (jax.nn.silu(gate_proj) * up_proj).astype(jnp.bfloat16)
    hidden = hidden.reshape(local_rows, gate_weight.shape[1], gate_weight.shape[2])
    down_all = lax.all_gather(down_weight, "row", axis=0, tiled=True)
    summed = jnp.einsum(
        "tgu,gud->td",
        lax.all_gather(hidden, "col", axis=2, tiled=True),
        down_all,
        preferred_element_type=jnp.float32,
    )
    return summed.astype(jnp.bfloat16)


def solution(mesh):
    in_specs = (
        P(("groups", "row"), "col"),
        P("row", None, "col"),
        P("row", None, "col"),
        P("row", None, "col"),
    )
    out_specs = P(("groups", "row"), "col")
    return jax.shard_map(local, mesh=mesh, in_specs=in_specs, out_specs=out_specs, check_vma=False)
```

profile of v0, /device:TPU:0, one launch (start us, length us, event | category | flops | bytes accessed | tf_op | source)
XLA Modules:
  0.0 471.2 jit_solution(7375806177939353306)
XLA Ops:
  6.5 0.0 all-gather.6.cloned.1.call-start
  6.5 0.7 all-gather.6.cloned.1.call-update
  7.3 0.0 all-gather.8.cloned.1.call-start
  7.3 19.3 %copy.8 = bf16[512,8,2,1664]{3,1,2,0:T(8,128)(2,1)} copy(bf16[512,8,2,1664]{3,2,1,0:T(2,128)(2,1)} %bitcast.20) | data formatting | bytes 54525952
  26.6 0.0 all-gather.8.cloned.1.call-update
  26.7 0.0 all-gather.10.cloned.1.call-start
  26.7 19.2 %copy.9 = bf16[512,8,2,1664]{3,1,2,0:T(8,128)(2,1)} copy(bf16[512,8,2,1664]{3,2,1,0:T(2,128)(2,1)} %bitcast.21) | data formatting | bytes 54525952
  45.9 0.0 all-gather.10.cloned.1.call-update
  46.0 0.0 all-gather.14.cloned.1.call-start
  46.0 0.5 all-gather.14.cloned.1.call-update
  46.5 0.0 all-gather.12.cloned.1.call-start
  46.6 20.4 %all-gather.6.cloned.1.call-done = bf16[160,8192]{1,0:T(8,128)(2,1)} async-done(((bf16[160,1024]{1,0:T(8,128)(2,1)}), bf16[160,8192]{1,0:T(8,128)(2,1)}) %all-gather.6.cloned.1.call-update) | async-done | bytes 2621456 | tf_op jit(solution)/shard_map/all_gather | solution.py:8
  66.9 0.0 copy-start
  66.9 79.9 %all-gather.8.cloned.1.call-done = bf16[8192,3328]{1,0:T(8,128)(2,1)} async-done(((bf16[4096,3328]{1,0:T(8,128)(2,1)}), bf16[8192,3328]{1,0:T(8,128)(2,1)}) %all-gather.8.cloned.1.call-update) | async-done | bytes 54525968 | tf_op jit(solution)/shard_map/all_gather | solution.py:14
  146.8 32.7 %fusion.2 = f32[160,3328]{1,0:T(8,128)} fusion(bf16[160,8192]{1,0:T(8,128)(2,1)} %all-gather.6.cloned.1.call-done, bf16[8192,3328]{1,0:T(8,128)(2,1)} %all-gather.8.cloned.1.call-done), kind=kOutput, calls=%fused_computation.5 | convolution fusion | flops 8724152320 | bytes 59277312 | tf_op jit(solution)/shard_map/dot_general | solution.py:12
  179.6 49.8 %all-gather.10.cloned.1.call-done = bf16[8192,3328]{1,0:T(8,128)(2,1)} async-done(((bf16[4096,3328]{1,0:T(8,128)(2,1)}), bf16[8192,3328]{1,0:T(8,128)(2,1)}) %all-gather.10.cloned.1.call-update) | async-done | bytes 54525968 | tf_op jit(solution)/shard_map/all_gather | solution.py:19
  229.4 0.0 copy-done
  229.4 30.5 %fusion = bf16[160,3328]{1,0:T(8,128)(2,1)S(1)} fusion(bf16[160,8192]{1,0:T(8,128)(2,1)S(1)} %copy-done, bf16[8192,3328]{1,0:T(8,128)(2,1)} %all-gather.10.cloned.1.call-done, f32[160,3328]{1,0:T(8,128)} %fusion.2), kind=kOutput, calls=%fused_computation.1 | convolution fusion | flops 8727347200 | bytes 60342272 | tf_op jit(solution)/shard_map/dot_general | solution.py:17
  259.9 1.1 copy.11
  260.9 0.0 all-gather.12.cloned.1.call-update
  261.0 50.8 %all-gather.14.cloned.1.call-done = bf16[2,13312,1024]{2,1,0:T(8,128)(2,1)} async-done(((bf16[1,13312,1024]{2,1,0:T(8,128)(2,1)}), bf16[2,13312,1024]{2,1,0:T(8,128)(2,1)}) %all-gather.14.cloned.1.call-update) | async-done | bytes 54525968 | tf_op jit(solution)/shard_map/all_gather | solution.py:24
  311.7 129.8 %all-gather.12.cloned.1.call-done = bf16[160,2,13312]{2,0,1:T(8,128)(2,1)} async-done(((bf16[160,2,1664]{2,0,1:T(8,128)(2,1)}), bf16[160,2,13312]{2,0,1:T(8,128)(2,1)}) %all-gather.12.cloned.1.call-update) | async-done | bytes 8519696 | tf_op jit(solution)/shard_map/all_gather | solution.py:27
  441.5 23.2 %fusion.1 = bf16[160,1024]{1,0:T(8,128)(2,1)} fusion(bf16[160,2,13312]{2,0,1:T(8,128)(2,1)} %all-gather.12.cloned.1.call-done, bf16[2,13312,1024]{2,1,0:T(8,128)(2,1)} %all-gather.14.cloned.1.call-done), kind=kOutput, calls=%fused_computation.3 | convolution fusion | flops 8724316160 | bytes 63373312 | tf_op jit(solution)/shard_map/tgu,gud->td/dot_general | solution.py:25
Async XLA Ops:
  6.5 60.4 %all-gather.6.cloned.1.call-start = ((), (), s32[]{:S(2)}) async-start(), calls=%async_computation | async-start | bytes 2949120 | tf_op jit(solution)/shard_map/all_gather | solution.py:8
  7.3 139.6 %all-gather.8.cloned.1.call-start = ((), (), s32[]{:S(2)}) async-start(), calls=%async_computation.1 | async-start | bytes 81788928 | tf_op jit(solution)/shard_map/all_gather | solution.py:14
  26.7 202.7 %all-gather.10.cloned.1.call-start = ((), (), s32[]{:S(2)}) async-start(), calls=%async_computation.2 | async-start | bytes 81788928 | tf_op jit(solution)/shard_map/all_gather | solution.py:19
  46.0 265.8 %all-gather.14.cloned.1.call-start = ((), (), s32[]{:S(2)}) async-start(), calls=%async_computation.4 | async-start | bytes 81788928 | tf_op jit(solution)/shard_map/all_gather | solution.py:24
  46.5 395.0 %all-gather.12.cloned.1.call-start = ((), (), s32[]{:S(2)}) async-start(), calls=%async_computation.3 | async-start | bytes 9584640 | tf_op jit(solution)/shard_map/all_gather | solution.py:27
  66.9 162.4 %copy-start = (bf16[160,8192]{1,0:T(8,128)(2,1)S(1)}, bf16[160,8192]{1,0:T(8,128)(2,1)}, u32[]{:S(2)}) copy-start(bf16[160,8192]{1,0:T(8,128)(2,1)} %all-gather.6.cloned.1.call-done) | copy-start | bytes 7864324
Sparse Core Ops, SparseCore 0:
  9.5 57.3 all-gather.5
  68.5 78.3 all-gather.7
  148.4 80.8 all-gather.9
  230.8 80.8 all-gather.13
  313.8 127.6 all-gather.11
where the time goes:
time: 471 us
  waiting for transfers between devices  332 us (70%)
  matrix products  86.4 us (18%)
  local copies, waits for them, and re-layouts  39.6 us (8%)
  between operations  13.1 us (3%)
    all_gather x1, waiting for transfers between devices, local(): lax.all_gather(hidden, 'col', axis=2, tiled=True)  130 us
    all_gather x1, waiting for transfers between devices, local(): lax.all_gather(gate_local, 'row', axis=0, tiled=True)  79.9 us
    all_gather x1, waiting for transfers between devices, local(): down_all = lax.all_gather(down_weight, 'row', axis=0, tiled=True)  50.8 us
    all_gather x1, waiting for transfers between devices, local(): lax.all_gather(up_local, 'row', axis=0, tiled=True)  49.8 us
    unnamed x4, local copies, waits for them, and re-layouts  38.6 us
    dot_general x1, matrix products, local(): jnp.dot(features, lax.all_gather(gate_local, 'row', axis=0, tiled=True),...  32.7 us
    dot_general x1, matrix products, local(): jnp.dot(features, lax.all_gather(up_local, 'row', axis=0, tiled=True), pr...  30.5 us
    dot_general x1, matrix products, local(): jnp.einsum('tgu,gud->td', lax.all_gather(hidden, 'col', axis=2, tiled=Tru...  23.2 us
  transfers between devices with their start and end apart: 5, of which 5 were waited for; matrix products, arithmetic and copies ran while one was open for 22% of the time, Pallas kernels for 0%

commit v1 on v0

v1 whole, which is shorter than its diff:
```python
import functools

import jax
import jax.numpy as jnp
from jax import lax
from jax.experimental import pallas as pl
from jax.experimental.pallas import tpu as pltpu
from jax.sharding import PartitionSpec as P

BF16, F32 = jnp.bfloat16, jnp.float32
LANES = 128
TOK_PARTS = 2
W_SLOTS = 3
D_SLOTS = 4
STEP = 512


def plain(tokens, gate_weight, up_weight, down_weight):
    row = lax.axis_index("row")
    features = lax.all_gather(tokens, "col", axis=1, tiled=True)
    features = lax.all_gather(features, "row", axis=0, tiled=True)
    depth = gate_weight.shape[0]
    features = lax.dynamic_slice_in_dim(features, row * depth, depth, 1)

    def project(weight):
        part = jnp.einsum("td,dbu->btu", features, weight, preferred_element_type=F32)
        return lax.psum_scatter(part, "row", scatter_dimension=0, tiled=True)[0]

    hidden = (jax.nn.silu(project(gate_weight)) * project(up_weight)).astype(BF16)
    hidden = lax.all_gather(hidden, "col", axis=1, tiled=True)
    part = jnp.dot(hidden, down_weight[0], preferred_element_type=F32)
    return lax.psum_scatter(part, "row", scatter_dimension=0, tiled=True).astype(BF16)


def kernel(n_z, chunks, tok_ref, gate_ref, up_ref, down_ref, out_ref,
           tokr, tokp, spread, wg, wu, pacc, own, psend, precv, hid, acc, wd, osend, orecv,
           w_sem, tp_send, tp_recv, tr_send, tr_recv, p_send, p_recv, h_send, h_recv, d_sem, o_send, o_recv, own_sem):
    col, r = lax.axis_index("col"), lax.axis_index("row")
    z, x = col // 2, col % 2
    peer = 1 - r
    above, below, across = col + 2, col - 2, z * 2 + 1 - x
    has_up, has_down = z < n_z - 1, z > 0
    rows = tok_ref.shape[0]
    both = 2 * rows
    wide = tok_ref.shape[1]
    piece = wide // TOK_PARTS
    half = n_z
    depth = gate_ref.shape[0]
    mesh_id = pl.DeviceIdType.MESH

    def weight_copies(k):
        slot = lax.rem(k, W_SLOTS)
        cols = pl.ds(pl.multiple_of(k * LANES, LANES), LANES)
        return (pltpu.make_async_copy(gate_ref.at[:, :, cols], wg.at[slot], w_sem.at[slot, 0]),
                pltpu.make_async_copy(up_ref.at[:, :, cols], wu.at[slot], w_sem.at[slot, 1]))

    for k in range(W_SLOTS - 1):
        for copy in weight_copies(jnp.int32(k)):
            copy.start()

    barrier = pltpu.get_barrier_semaphore()
    pl.semaphore_signal(barrier, inc=1, device_id={"row": peer}, device_id_type=mesh_id)
    pl.semaphore_signal(barrier, inc=1, device_id={"col": across}, device_id_type=mesh_id)

    @pl.when(has_up)
    def _():
        pl.semaphore_signal(barrier, inc=1, device_id={"col": above}, device_id_type=mesh_id)

    @pl.when(has_down)
    def _():
        pl.semaphore_signal(barrier, inc=1, device_id={"col": below}, device_id_type=mesh_id)

    pl.semaphore_wait(barrier, 2 + has_up.astype(jnp.int32) + has_down.astype(jnp.int32))

    def block(buf, send, recv, unit, k, way, to):
        return pltpu.make_async_remote_copy(
            src_ref=buf.at[unit, k], dst_ref=buf.at[unit, k], send_sem=send.at[way, k],
            recv_sem=recv.at[unit, k], device_id={"col": to}, device_id_type=mesh_id)

    UP, DOWN, XL, XU = 0, 1, 2, 3

    def send_own(buf, send, recv, k):
        @pl.when(has_up)
        def _():
            block(buf, send, recv, col, k, UP, above).start()

        @pl.when(has_down)
        def _():
            block(buf, send, recv, col, k, DOWN, below).start()

        block(buf, send, recv, col, k, XL, across).start()

    def relay(buf, send, recv, s, k, arrived):
        lower, upper = col - 2 * s, col + 2 * s

        @pl.when(z - s >= 0)
        def _():
            block(buf, send, recv, lower, k, XL, across).wait_recv()

            @pl.when(has_up)
            def _():
                copy = block(buf, send, recv, lower, k, UP, above)
                copy.wait_send()
                copy.start()

            copy = block(buf, send, recv, lower, k, XL, across)
            copy.wait_send()
            copy.start()
            arrived(lower, k, 0)

        @pl.when(z + s < n_z)
        def _():
            block(buf, send, recv, upper, k, XU, across).wait_recv()

            @pl.when(has_down)
            def _():
                copy = block(buf, send, recv, upper, k, DOWN, below)
                copy.wait_send()
                copy.start()

            copy = block(buf, send, recv, upper, k, XU, across)

            @pl.when(s > 1)
            def _():
                copy.wait_send()

            copy.start()
            arrived(upper, k, 1)

        t = s - 1
        xl, xu = across - 2 * t, across + 2 * t

        @pl.when(z - t >= 0)
        def _():
            block(buf, send, recv, xl, k, XL, across).wait_recv()
            arrived(xl, k, 2)

        @pl.when((t > 0) & (z + t < n_z))
        def _():
            block(buf, send, recv, xu, k, XL, across).wait_recv()
            arrived(xu, k, 3)

    def drain(buf, send, recv, k):
        @pl.when(has_up)
        def _():
            block(buf, send, recv, col, k, UP, above).wait_send()
            block(buf, send, recv, col, k, XU, across).wait_send()

        @pl.when(has_down)
        def _():
            block(buf, send, recv, col, k, DOWN, below).wait_send()

        block(buf, send, recv, col, k, XL, across).wait_send()

    def to_peer(unit, k):
        at = lax.rem(unit, half)
        return pltpu.make_async_remote_copy(
            src_ref=tokr.at[unit, k], dst_ref=tokp.at[at, k], send_sem=tp_send.at[at, k],
            recv_sem=tp_recv.at[at, k], device_id={"row": peer}, device_id_type=mesh_id)

    def token_arrived(unit, k, j):
        @pl.when(unit // half != r)
        def _():
            to_peer(unit, k).start()

    for k in range(TOK_PARTS):
        copy = pltpu.make_async_copy(tok_ref.at[:, pl.ds(k * piece, piece)], tokr.at[col, k], own_sem.at[k])
        copy.start()
    for k in range(TOK_PARTS):
        pltpu.make_async_copy(tok_ref.at[:, pl.ds(k * piece, piece)], tokr.at[col, k], own_sem.at[k]).wait()
        send_own(tokr, tr_send, tr_recv, k)
        token_arrived(col, k, 0)

    def token_step(i, carry):
        relay(tokr, tr_send, tr_recv, i // TOK_PARTS + 1, lax.rem(i, TOK_PARTS), token_arrived)
        return carry

    lax.fori_loop(0, n_z * TOK_PARTS, token_step, 0)

    source = lax.broadcasted_iota(jnp.int32, (LANES, 2 * LANES), 0)
    place = lax.broadcasted_iota(jnp.int32, (LANES, 2 * LANES), 1)
    picks = [jnp.where(place == 2 * source + b, 1.0, 0.0).astype(BF16) for b in range(2)]

    def spread_rows(src, at, k, first):
        for j in range(piece // LANES):
            value = src[:, j * LANES:(j + 1) * LANES]
            dst = pl.multiple_of(((at * TOK_PARTS + k) * (piece // LANES) + j) * 2 * LANES, 2 * LANES)
            for b in range(2):
                spread[pl.ds(pl.multiple_of(b * both + first, 16), rows), pl.ds(dst, 2 * LANES)] = jnp.dot(
                    value, picks[b], preferred_element_type=F32).astype(BF16)

    def spread_step(i, carry):
        at, k = i // TOK_PARTS, lax.rem(i, TOK_PARTS)
        unit = r * half + at
        spread_rows(tokr.at[unit, k], at, k, r * rows)
        to_peer(unit, k).wait_recv()
        spread_rows(tokp.at[at, k], at, k, peer * rows)
        to_peer(unit, k).wait_send()
        return carry

    lax.fori_loop(0, half * TOK_PARTS, spread_step, 0)
    for k in range(TOK_PARTS):
        drain(tokr, tr_send, tr_recv, k)

    def partial(k):
        return pltpu.make_async_remote_copy(
            src_ref=psend.at[k], dst_ref=precv.at[k], send_sem=p_send.at[k], recv_sem=p_recv.at[k],
            device_id={"row": peer}, device_id_type=mesh_id)

    def make_step(k, carry):
        @pl.when(k < chunks)
        def _():
            slot = lax.rem(k, W_SLOTS)

            @pl.when(k + W_SLOTS - 1 < chunks)
            def _():
                for copy in weight_copies(k + W_SLOTS - 1):
                    copy.start()

            for copy in weight_copies(k):
                copy.wait()
            pacc[...] = jnp.zeros_like(pacc)

            def contract(i, c):
                at = pl.ds(pl.multiple_of(i * STEP, STEP), STEP)
                gate = wg[slot, at].reshape(2 * STEP, LANES)
                up = wu[slot, at].reshape(2 * STEP, LANES)
                pacc[...] += jnp.dot(
                    spread[:, pl.ds(pl.multiple_of(i * 2 * STEP, 2 * STEP), 2 * STEP)],
                    jnp.concatenate([gate, up], axis=1), preferred_element_type=F32)
                return c

            lax.fori_loop(0, depth // STEP, contract, 0)
            psend[k] = pacc[pl.ds(pl.multiple_of(peer * both, 16), both), :].astype(BF16)
            partial(k).start()

        @pl.when(k > 0)
        def _():
            last = k - 1
            partial(last).wait_recv()
            total = own[...] + precv[last].astype(F32)
            gate, up = total[:, :LANES], total[:, LANES:]
            hid[col, last] = (gate / (1.0 + jnp.exp(-gate)) * up).astype(BF16)
            send_own(hid, h_send, h_recv, last)

        @pl.when(k < chunks)
        def _():
            own[...] = pacc[pl.ds(pl.multiple_of(r * both, 16), both), :]

        return carry

    lax.fori_loop(0, chunks + 1, make_step, 0)

    steps = n_z * chunks

    def unit_of(s, j):
        t = s - 1
        if j == 0:
            return z - s >= 0, col - 2 * s
        if j == 1:
            return z + s < n_z, col + 2 * s
        if j == 2:
            return z - t >= 0, across - 2 * t
        first = t == 0
        return first | (z + t < n_z), jnp.where(first, col, across + 2 * t)

    def down_copy(unit, k, slot, j):
        at = pl.multiple_of((unit * chunks + k) * LANES, LANES)
        return pltpu.make_async_copy(down_ref.at[0, pl.ds(at, LANES), :], wd.at[slot, j], d_sem.at[slot, j])

    def fetch(i):
        s, k = i // chunks + 1, lax.rem(i, chunks)
        for j in range(4):
            valid, unit = unit_of(s, j)

            @pl.when(valid)
            def _(unit=unit, j=j):
                down_copy(unit, k, lax.rem(i, D_SLOTS), j).start()

    for i in range(D_SLOTS - 1):
        fetch(jnp.int32(i))
    acc[...] = jnp.zeros_like(acc)

    def down_step(i, carry):
        s, k = i // chunks + 1, lax.rem(i, chunks)
        slot = lax.rem(i, D_SLOTS)

        @pl.when(i + D_SLOTS - 1 < steps)
        def _():
            fetch(i + D_SLOTS - 1)

        def arrived(unit, k, j):
            down_copy(unit, k, slot, j).wait()
            acc[...] += jnp.dot(hid[unit, k], wd[slot, j], preferred_element_type=F32)

        relay(hid, h_send, h_recv, s, k, arrived)

        @pl.when(s == 1)
        def _():
            arrived(col, k, 3)

        return carry

    lax.fori_loop(0, steps, down_step, 0)

    osend[...] = acc[pl.ds(pl.multiple_of(peer * rows, 16), rows), :].astype(BF16)
    copy = pltpu.make_async_remote_copy(
        src_ref=osend, dst_ref=orecv, send_sem=o_send, recv_sem=o_recv,
        device_id={"row": peer}, device_id_type=mesh_id)
    copy.start()

    def finish(k, carry):
        drain(hid, h_send, h_recv, k)
        partial(k).wait_send()
        return carry

    lax.fori_loop(0, chunks, finish, 0)
    copy.wait()
    out_ref[...] = (acc[pl.ds(pl.multiple_of(r * rows, 16), rows), :] + orecv[...].astype(F32)).astype(BF16)


def fused(n_col, tokens, gate_weight, up_weight, down_weight):
    rows, wide = tokens.shape
    depth, _, units = gate_weight.shape
    chunks = units // LANES
    n_z = n_col // 2
    both = 2 * rows
    any_space = pl.BlockSpec(memory_space=pl.ANY)
    vmem = pl.BlockSpec(memory_space=pltpu.VMEM)
    dma = pltpu.SemaphoreType.DMA
    return pl.pallas_call(
        functools.partial(kernel, n_z, chunks),
        out_shape=jax.ShapeDtypeStruct((rows, down_weight.shape[2]), BF16),
        in_specs=[any_space] * 4,
        out_specs=vmem,
        scratch_shapes=[
            pltpu.VMEM((n_col, TOK_PARTS, rows, wide // TOK_PARTS), BF16),
            pltpu.VMEM((n_z, TOK_PARTS, rows, wide // TOK_PARTS), BF16),
            pltpu.VMEM((2 * both, 2 * depth), BF16),
            pltpu.VMEM((W_SLOTS, depth, 2, LANES), BF16),
            pltpu.VMEM((W_SLOTS, depth, 2, LANES), BF16),
            pltpu.VMEM((2 * both, 2 * LANES), F32),
            pltpu.VMEM((both, 2 * LANES), F32),
            pltpu.VMEM((chunks, both, 2 * LANES), BF16),
            pltpu.VMEM((chunks, both, 2 * LANES), BF16),
            pltpu.VMEM((n_col, chunks, both, LANES), BF16),
            pltpu.VMEM((both, down_weight.shape[2]), F32),
            pltpu.VMEM((D_SLOTS, 4, LANES, down_weight.shape[2]), BF16),
            pltpu.VMEM((rows, down_weight.shape[2]), BF16),
            pltpu.VMEM((rows, down_weight.shape[2]), BF16),
            dma((W_SLOTS, 2)),
            dma((n_z, TOK_PARTS)), dma((n_z, TOK_PARTS)),
            dma((4, TOK_PARTS)), dma((n_col, TOK_PARTS)),
            dma((chunks,)), dma((chunks,)),
            dma((4, chunks)), dma((n_col, chunks)),
            dma((D_SLOTS, 4)),
            dma, dma,
            dma((TOK_PARTS,)),
        ],
        compiler_params=pltpu.CompilerParams(
            collective_id=0, has_side_effects=True, vmem_limit_bytes=58 * 2**20),
    )(tokens, gate_weight, up_weight, down_weight)


def solution(mesh):
    n_col = mesh.shape["col"]

    def local(tokens, gate_weight, up_weight, down_weight):
        rows, wide = tokens.shape
        depth, blocks, units = gate_weight.shape
        fits = (n_col == 8 and mesh.shape["row"] == 2 and blocks == 2 and units % LANES == 0
                and rows % 16 == 0 and wide % (TOK_PARTS * LANES) == 0 and depth % STEP == 0
                and 2 * depth == n_col * wide)
        if fits:
            return fused(n_col, tokens, gate_weight, up_weight, down_weight)
        return plain(tokens, gate_weight, up_weight, down_weight)

    in_specs = (
        P(("groups", "row"), "col"),
        P("row", None, "col"),
        P("row", None, "col"),
        P("row", None, "col"),
    )
    out_specs = P(("groups", "row"), "col")
    return jax.shard_map(local, mesh=mesh, in_specs=in_specs, out_specs=out_specs, check_vma=False)
```

time: 471 us -> 185 us (0.39)
  waiting for transfers between devices: 332 us -> 0 us
  Pallas kernels: 0 us -> 182 us
  matrix products: 86.4 us -> 0 us
  local copies, waits for them, and re-layouts: 39.6 us -> 1.72 us
  between operations: 13.1 us -> 0.01 us
    all_gather x5 -> x0, waiting for transfers between devices: 331 us -> none  [the longest x1 130 us: local(): lax.all_gather(hidden, 'col', axis=2, tiled=True)]
    pallas_call x0 -> x1, Pallas kernels: none -> 182 us  [fused(): pl.pallas_call(functools.partial(kernel, n_z, chunks), out_shape=jax.Shap...]
    dot_general x3 -> x0, matrix products: 86.4 us -> none  [the longest x1 32.7 us: local(): jnp.dot(features, lax.all_gather(gate_local, 'row', axis=0, tiled=True),...]
    unnamed x4 -> x1, local copies, waits for them, and re-layouts: 38.6 us -> 1.72 us
  transfers between devices with their start and end apart: 5 -> 0, of which waited for: 5 -> 0; matrix products, arithmetic and copies ran while one was open for 22% -> 0% of each run, Pallas kernels for 0% -> 0%
where the time goes in v1:
time: 185 us; the launch traced here: 184 us
  Pallas kernels  182 us (98%)
    pallas_call x1, Pallas kernels, fused(): pl.pallas_call(functools.partial(kernel, n_z, chunks), out_shape=jax.Shap...  182 us

profile of v1, /device:TPU:0, one launch (start us, length us, event | category | flops | bytes accessed | tf_op | source)
XLA Modules:
  0.0 183.9 jit_solution(10624692358183853497)
XLA Ops:
  0.0 182.2 %shard_map.46 = bf16[160,1024]{1,0:T(8,128)(2,1)} custom-call(bf16[160,1024]{1,0:T(8,128)(2,1)} %tok_ref.1, bf16[4096,2,1664]{2,1,0:T(2,128)(2,1)} %gate_ref.1, bf16[4096,2,1664]{2,1,0:T(2,128)(2,1)} %up_ref.1, bf16[1,13312,1024]{2,1,0:T(8,128)(2,1)} %down_ref.1), custom_call_target="tpu_custom_call" | custom-call | tf_op jit(solution)/shard_map/pallas_call | solution.py:331
  182.2 1.7 copy.6

commit v2 on v1

--- a/solution.py
+++ b/solution.py
@@ -12,7 +12,9 @@
 TOK_PARTS = 2
 W_SLOTS = 3
 D_SLOTS = 4
-STEP = 512
+ACROSS = 2
+LAG = 2
+STEP = 4096
 
 
 def plain(tokens, gate_weight, up_weight, down_weight):
@@ -77,7 +79,7 @@
             src_ref=buf.at[unit, k], dst_ref=buf.at[unit, k], send_sem=send.at[way, k],
             recv_sem=recv.at[unit, k], device_id={"col": to}, device_id_type=mesh_id)
 
-    UP, DOWN, XL, XU = 0, 1, 2, 3
+    UP, DOWN, XL, XU, UP2, DOWN2 = 0, 1, 2, 3, 4, 5
 
     def send_own(buf, send, recv, k):
         @pl.when(has_up)
@@ -90,7 +92,7 @@
 
         block(buf, send, recv, col, k, XL, across).start()
 
-    def relay(buf, send, recv, s, k, arrived):
+    def relay(buf, send, recv, s, k, arrived, turned):
         lower, upper = col - 2 * s, col + 2 * s
 
         @pl.when(z - s >= 0)
@@ -103,9 +105,12 @@
                 copy.wait_send()
                 copy.start()
 
-            copy = block(buf, send, recv, lower, k, XL, across)
-            copy.wait_send()
-            copy.start()
+            @pl.when(k >= turned)
+            def _():
+                copy = block(buf, send, recv, lower, k, XL, across)
+                copy.wait_send()
+                copy.start()
+
             arrived(lower, k, 0)
 
         @pl.when(z + s < n_z)
@@ -118,13 +123,16 @@
                 copy.wait_send()
                 copy.start()
 
-            copy = block(buf, send, recv, upper, k, XU, across)
-
-            @pl.when(s > 1)
-            def _():
-                copy.wait_send()
-
-            copy.start()
+            @pl.when(k >= turned)
+            def _():
+                copy = block(buf, send, recv, upper, k, XU, across)
+
+                @pl.when(s > 1)
+                def _():
+                    copy.wait_send()
+
+                copy.start()
+
             arrived(upper, k, 1)
 
         t = s - 1
@@ -133,22 +141,55 @@
         @pl.when(z - t >= 0)
         def _():
             block(buf, send, recv, xl, k, XL, across).wait_recv()
+
+            @pl.when((k < turned) & has_up)
+            def _():
+                copy = block(buf, send, recv, xl, k, UP2, above)
+
+                @pl.when(t > 0)
+                def _():
+                    copy.wait_send()
+
+                copy.start()
+
+            @pl.when((k < turned) & has_down & (t == 0))
+            def _():
+                block(buf, send, recv, xl, k, DOWN2, below).start()
+
             arrived(xl, k, 2)
 
         @pl.when((t > 0) & (z + t < n_z))
         def _():
             block(buf, send, recv, xu, k, XL, across).wait_recv()
+
+            @pl.when((k < turned) & has_down)
+            def _():
+                copy = block(buf, send, recv, xu, k, DOWN2, below)
+                copy.wait_send()
+                copy.start()
+
             arrived(xu, k, 3)
 
-    def drain(buf, send, recv, k):
+    def drain(buf, send, recv, k, turned):
         @pl.when(has_up)
         def _():
             block(buf, send, recv, col, k, UP, above).wait_send()
+
+        @pl.when(has_up & (k >= turned))
+        def _():
             block(buf, send, recv, col, k, XU, across).wait_send()
 
+        @pl.when(has_up & (k < turned))
+        def _():
+            block(buf, send, recv, col, k, UP2, above).wait_send()
+
         @pl.when(has_down)
         def _():
             block(buf, send, recv, col, k, DOWN, below).wait_send()
+
+        @pl.when(has_down & (k < turned))
+        def _():
+            block(buf, send, recv, col, k, DOWN2, below).wait_send()
 
         block(buf, send, recv, col, k, XL, across).wait_send()
 
@@ -172,7 +213,7 @@
         token_arrived(col, k, 0)
 
     def token_step(i, carry):
-        relay(tokr, tr_send, tr_recv, i // TOK_PARTS + 1, lax.rem(i, TOK_PARTS), token_arrived)
+        relay(tokr, tr_send, tr_recv, i // TOK_PARTS + 1, lax.rem(i, TOK_PARTS), token_arrived, 0)
         return carry
 
     lax.fori_loop(0, n_z * TOK_PARTS, token_step, 0)
@@ -200,56 +241,7 @@
 
     lax.fori_loop(0, half * TOK_PARTS, spread_step, 0)
     for k in range(TOK_PARTS):
-        drain(tokr, tr_send, tr_recv, k)
-
-    def partial(k):
-        return pltpu.make_async_remote_copy(
-            src_ref=psend.at[k], dst_ref=precv.at[k], send_sem=p_send.at[k], recv_sem=p_recv.at[k],
-            device_id={"row": peer}, device_id_type=mesh_id)
-
-    def make_step(k, carry):
-        @pl.when(k < chunks)
-        def _():
-            slot = lax.rem(k, W_SLOTS)
-
-            @pl.when(k + W_SLOTS - 1 < chunks)
-            def _():
-                for copy in weight_copies(k + W_SLOTS - 1):
-                    copy.start()
-
-            for copy in weight_copies(k):
-                copy.wait()
-            pacc[...] = jnp.zeros_like(pacc)
-
-            def contract(i, c):
-                at = pl.ds(pl.multiple_of(i * STEP, STEP), STEP)
-                gate = wg[slot, at].reshape(2 * STEP, LANES)
-                up = wu[slot, at].reshape(2 * STEP, LANES)
-                pacc[...] += jnp.dot(
-                    spread[:, pl.ds(pl.multiple_of(i * 2 * STEP, 2 * STEP), 2 * STEP)],
-                    jnp.concatenate([gate, up], axis=1), preferred_element_type=F32)
-                return c
-
-            lax.fori_loop(0, depth // STEP, contract, 0)
-            psend[k] = pacc[pl.ds(pl.multiple_of(peer * both, 16), both), :].astype(BF16)
-            partial(k).start()
-
-        @pl.when(k > 0)
-        def _():
-            last = k - 1
-            partial(last).wait_recv()
-            total = own[...] + precv[last].astype(F32)
-            gate, up = total[:, :LANES], total[:, LANES:]
-            hid[col, last] = (gate / (1.0 + jnp.exp(-gate)) * up).astype(BF16)
-            send_own(hid, h_send, h_recv, last)
-
-        @pl.when(k < chunks)
-        def _():
-            own[...] = pacc[pl.ds(pl.multiple_of(r * both, 16), both), :]
-
-        return carry
-
-    lax.fori_loop(0, chunks + 1, make_step, 0)
+        drain(tokr, tr_send, tr_recv, k, 0)
 
     steps = n_z * chunks
 
@@ -293,7 +285,7 @@
             down_copy(unit, k, slot, j).wait()
             acc[...] += jnp.dot(hid[unit, k], wd[slot, j], preferred_element_type=F32)
 
-        relay(hid, h_send, h_recv, s, k, arrived)
+        relay(hid, h_send, h_recv, s, k, arrived, ACROSS)
 
         @pl.when(s == 1)
         def _():
@@ -301,7 +293,59 @@
 
         return carry
 
-    lax.fori_loop(0, steps, down_step, 0)
+    def partial(k):
+        return pltpu.make_async_remote_copy(
+            src_ref=psend.at[k], dst_ref=precv.at[k], send_sem=p_send.at[k], recv_sem=p_recv.at[k],
+            device_id={"row": peer}, device_id_type=mesh_id)
+
+    def make_step(k, carry):
+        @pl.when(k < chunks)
+        def _():
+            slot = lax.rem(k, W_SLOTS)
+
+            @pl.when(k + W_SLOTS - 1 < chunks)
+            def _():
+                for copy in weight_copies(k + W_SLOTS - 1):
+                    copy.start()
+
+            for copy in weight_copies(k):
+                copy.wait()
+            pacc[...] = jnp.zeros_like(pacc)
+
+            def contract(i, c):
+                at = pl.ds(pl.multiple_of(i * STEP, STEP), STEP)
+                gate = wg[slot, at].reshape(2 * STEP, LANES)
+                up = wu[slot, at].reshape(2 * STEP, LANES)
+                pacc[...] += jnp.dot(
+                    spread[:, pl.ds(pl.multiple_of(i * 2 * STEP, 2 * STEP), 2 * STEP)],
+                    jnp.concatenate([gate, up], axis=1), preferred_element_type=F32)
+                return c
+
+            lax.fori_loop(0, depth // STEP, contract, 0)
+            psend[k] = pacc[pl.ds(pl.multiple_of(peer * both, 16), both), :].astype(BF16)
+            partial(k).start()
+
+        @pl.when(k > 0)
+        def _():
+            last = k - 1
+            partial(last).wait_recv()
+            total = own[...] + precv[last].astype(F32)
+            gate, up = total[:, :LANES], total[:, LANES:]
+            hid[col, last] = (gate / (1.0 + jnp.exp(-gate)) * up).astype(BF16)
+            send_own(hid, h_send, h_recv, last)
+
+        @pl.when(k < chunks)
+        def _():
+            own[...] = pacc[pl.ds(pl.multiple_of(r * both, 16), both), :]
+
+        @pl.when(k > LAG)
+        def _():
+            down_step(k - 1 - LAG, 0)
+
+        return carry
+
+    lax.fori_loop(0, chunks + 1, make_step, 0)
+    lax.fori_loop(chunks - LAG, steps, down_step, 0)
 
     osend[...] = acc[pl.ds(pl.multiple_of(peer * rows, 16), rows), :].astype(BF16)
     copy = pltpu.make_async_remote_copy(
@@ -310,7 +354,7 @@
     copy.start()
 
     def finish(k, carry):
-        drain(hid, h_send, h_recv, k)
+        drain(hid, h_send, h_recv, k, ACROSS)
         partial(k).wait_send()
         return carry
 
@@ -350,9 +394,9 @@
             pltpu.VMEM((rows, down_weight.shape[2]), BF16),
             dma((W_SLOTS, 2)),
             dma((n_z, TOK_PARTS)), dma((n_z, TOK_PARTS)),
-            dma((4, TOK_PARTS)), dma((n_col, TOK_PARTS)),
+            dma((6, TOK_PARTS)), dma((n_col, TOK_PARTS)),
             dma((chunks,)), dma((chunks,)),
-            dma((4, chunks)), dma((n_col, chunks)),
+            dma((6, chunks)), dma((n_col, chunks)),
             dma((D_SLOTS, 4)),
             dma, dma,
             dma((TOK_PARTS,)),

time: 185 us -> 151 us (0.82)
  Pallas kernels: 182 us -> 149 us
    pallas_call x1, Pallas kernels: 182 us -> 149 us  [fused(): pl.pallas_call(functools.partial(kernel, n_z, chunks), out_shape=jax.Shap...]
where the time goes in v2:
time: 151 us
  Pallas kernels  149 us (99%)
  local copies, waits for them, and re-layouts  1.72 us (1%)
    pallas_call x1, Pallas kernels, fused(): pl.pallas_call(functools.partial(kernel, n_z, chunks), out_shape=jax.Shap...  149 us

profile of v2, /device:TPU:0, one launch (start us, length us, event | category | flops | bytes accessed | tf_op | source)
XLA Modules:
  0.0 150.8 jit_solution(6734020389924045602)
XLA Ops:
  0.0 149.1 %shard_map.46 = bf16[160,1024]{1,0:T(8,128)(2,1)} custom-call(bf16[160,1024]{1,0:T(8,128)(2,1)} %tok_ref.1, bf16[4096,2,1664]{2,1,0:T(2,128)(2,1)} %gate_ref.1, bf16[4096,2,1664]{2,1,0:T(2,128)(2,1)} %up_ref.1, bf16[1,13312,1024]{2,1,0:T(8,128)(2,1)} %down_ref.1), custom_call_target="tpu_custom_call" | custom-call | tf_op jit(solution)/shard_map/pallas_call | solution.py:375
  149.1 1.7 %copy.6 = bf16[160,1024]{1,0:T(8,128)(2,1)} copy(bf16[160,1024]{1,0:T(8,128)(2,1)} %shard_map.46) | data formatting | bytes 655360
